TPU v7x, 256 devices: a whole 4x4x8 slice. The times are simulated.
256 devices in a mesh: tm: 16 (over x, y), space: 16 (over z, core).
Axes of the slice: x: 4, y: 4, z: 8, core: 2. Of those that a mesh axis runs over, the one named last changes fastest.
Arguments:
- queries: bfloat16 [32, 32, 32, 2240], P('tm', 'space'), may hold values from -6 to 6
- keys: bfloat16 [32, 32, 32, 2240], P('tm', 'space'), may hold values from -6 to 6
- values: bfloat16 [32, 32, 32, 2240], P('tm', 'space'), may hold values from -6 to 6
- out_grad: bfloat16 [32, 32, 32, 2240], P('tm', 'space'), may hold values from -6 to 6
- block_start: int32 [32], P('tm'), may hold values 0 or 1
- conv_input: bfloat16 [32, 32, 32, 5632], P('tm', 'space'), may hold values from -6 to 6
- conv_grad: bfloat16 [32, 32, 32, 5632], P('tm', 'space'), may hold values from -6 to 6
- conv_weight: float32 [9, 5632], replicated, may hold values from -2 to 2
Outputs:
- query_grad: bfloat16 [32, 32, 32, 2240], P('tm', 'space')
- key_grad: bfloat16 [32, 32, 32, 2240], P('tm', 'space')
- value_grad: bfloat16 [32, 32, 32, 2240], P('tm', 'space')
- input_grad: bfloat16 [32, 32, 32, 5632], P('tm', 'space')
- kernel_grad: float32 [9, 5632], replicated
All inputs are finite; a program needn't handle non-finite values. No bound on the sum of `block_start` on one device may be relied on, other than what follows from the above.
Results may differ from a plain program's by a relative error of at most 0.0088.
Values may be sent and summed in bfloat16 or wider, within the bound.
A program may use at most 128 MiB of HBM per device.

v0:
```python
import math
import jax
import jax.numpy as jnp
from jax import lax
from jax.sharding import PartitionSpec as P

HEADS = 20
HD = 112
highest = lax.Precision.HIGHEST


def with_halo(cells, sides, width):
    for axis, dim in sides:
        count = lax.axis_size(axis)
        ends = count - 1
        head = lax.slice_in_dim(cells, 0, width, axis=dim)
        tail = lax.slice_in_dim(cells, cells.shape[dim] - width, cells.shape[dim], axis=dim)
        cells = jnp.concatenate(
            [
                lax.ppermute(tail, axis, [(i, (i + 1) % count) for i in range(ends)]),
                cells,
                lax.ppermute(head, axis, [((i + 1) % count, i) for i in range(ends)]),
            ],
            axis=dim,
        )
    return cells


def prefix(part, axis, combine, identity, reverse):
    count = lax.axis_size(axis)
    place = lax.axis_index(axis)
    ahead = count - 1 - place if reverse else place
    gathered = jax.tree.map(lambda a: lax.all_gather(a, axis), part)
    state = jax.tree.map(lambda a, e: jnp.zeros_like(a) + jnp.asarray(e, a.dtype), part, identity)

    def one(turn, state):
        source = count - 1 - turn if reverse else turn
        return combine(
            state, jax.tree.map(lambda a: lax.dynamic_index_in_dim(a, source, 0, False), gathered)
        )

    return lax.fori_loop(0, ahead, one, state)


def lifted(x):
    widened = x.astype(jnp.float32)
    return jnp.where(widened > 0, widened + 1.0, jnp.exp(jnp.minimum(widened, 0.0)))


def slopes(x):
    widened = x.astype(jnp.float32)
    return jnp.where(widened > 0, 1.0, jnp.exp(jnp.minimum(widened, 0.0)))


def visibility(block_start, count):
    position = jnp.arange(count, dtype=jnp.int32)
    starts = jnp.where(position == 0, 1, block_start)
    block_ids = jnp.cumsum(starts)
    return (block_ids[None, :] <= block_ids[:, None]).astype(jnp.float32)


def add_pair(earlier, later):
    return (earlier[0] + later[0], earlier[1] + later[1])


def body(queries, keys, values, out_grad, block_start, conv_input, conv_grad, conv_weight):
    frames, rows, cols, width = queries.shape
    heads = HEADS
    depth = HD
    head_shape = (frames, rows * cols, heads, depth)
    q_feat = lifted(queries).astype(jnp.bfloat16).reshape(head_shape)
    k_feat = lifted(keys).astype(jnp.bfloat16).reshape(head_shape)
    v_heads = values.reshape(head_shape)
    visible = visibility(block_start, frames)
    rimmed = with_halo(conv_grad, (("space", 1),), 1)
    states = jnp.einsum("fnhd,fnhe->fhde", k_feat, v_heads, preferred_element_type=jnp.float32)
    sums = jnp.sum(k_feat.astype(jnp.float32), axis=1)
    states, sums = lax.psum((states, sums), "space")
    earlier = prefix(
        (jnp.sum(states, axis=0), jnp.sum(sums, axis=0)),
        "tm",
        add_pair,
        (jnp.zeros(states.shape[1:], jnp.float32), jnp.zeros(sums.shape[1:], jnp.float32)),
        False,
    )
    seen_states = jnp.einsum("fg,ghde->fhde", visible, states, precision=highest) + earlier[0][None]
    seen_sums = jnp.einsum("fg,ghd->fhd", visible, sums, precision=highest) + earlier[1][None]
    q_wide = q_feat.astype(jnp.float32)
    grad_wide = out_grad.reshape(head_shape).astype(jnp.float32)
    numer = jnp.einsum("fnhd,fhde->fnhe", q_wide, seen_states, precision=highest)
    denominator = jnp.einsum("fnhd,fhd->fnh", q_wide, seen_sums, precision=highest)
    output = numer / denominator[..., None]
    numer_grad = (grad_wide / denominator[..., None]).astype(jnp.bfloat16)
    denom_grad = -jnp.sum(grad_wide * output, axis=-1) / denominator
    q_grad = jnp.einsum(
        "fnhe,fhde->fnhd", numer_grad.astype(jnp.float32), seen_states, precision=highest
    )
    q_grad = (q_grad + denom_grad[..., None] * seen_sums[:, None]) * slopes(
        queries.reshape(head_shape)
    )
    grad_states = jnp.einsum(
        "fnhd,fnhe->fhde", q_feat, numer_grad, preferred_element_type=jnp.float32
    )
    grad_sums = jnp.einsum("fnhd,fnh->fhd", q_wide, denom_grad, precision=highest)
    grad_states, grad_sums = lax.psum((grad_states, grad_sums), "space")
    later = prefix(
        (jnp.sum(grad_states, axis=0), jnp.sum(grad_sums, axis=0)),
        "tm",
        add_pair,
        (
            jnp.zeros(grad_states.shape[1:], jnp.float32),
            jnp.zeros(grad_sums.shape[1:], jnp.float32),
        ),
        True,
    )
    seen_grads = (
        jnp.einsum("fg,fhde->ghde", visible, grad_states, precision=highest) + later[0][None]
    )
    seen_gsums = jnp.einsum("fg,fhd->ghd", visible, grad_sums, precision=highest) + later[1][None]
    k_grad = jnp.einsum(
        "fnhe,fhde->fnhd", v_heads.astype(jnp.float32), seen_grads, precision=highest
    )
    k_grad = (k_grad + seen_gsums[:, None]) * slopes(keys.reshape(head_shape))
    v_grad = jnp.einsum(
        "fnhd,fhde->fnhe", k_feat.astype(jnp.float32), seen_grads, precision=highest
    )
    out_shape = (frames, rows, cols, width)
    padded = jnp.pad(rimmed.astype(jnp.float32), ((0, 0), (0, 0), (1, 1), (0, 0)))
    input_wide = conv_input.astype(jnp.float32)
    accum = jnp.zeros(conv_grad.shape, jnp.float32)
    kernel_rows = []
    for i in range(3):
        for j in range(3):
            window = padded[:, 2 - i : 2 - i + rows, 2 - j : 2 - j + cols]
            accum = accum + conv_weight[3 * i + j] * window
            kernel_rows.append(jnp.sum(window * input_wide, axis=(0, 1, 2)))
    kernel_total = lax.psum(jnp.stack(kernel_rows), ("tm", "space"))
    tokens_all = frames * rows * cols * lax.axis_size("tm") * lax.axis_size("space")
    kernel_grad = kernel_total * (1.0 / math.sqrt(tokens_all))
    return (
        q_grad.astype(jnp.bfloat16).reshape(out_shape),
        k_grad.astype(jnp.bfloat16).reshape(out_shape),
        v_grad.astype(jnp.bfloat16).reshape(out_shape),
        accum.astype(jnp.bfloat16),
        kernel_grad,
    )


def solution(mesh):
    placed = (
        P("tm", "space", None, None),
        P("tm", "space", None, None),
        P("tm", "space", None, None),
        P("tm", "space", None, None),
        P("tm"),
        P("tm", "space", None, None),
        P("tm", "space", None, None),
        P(),
    )
    return jax.shard_map(
        body,
        mesh=mesh,
        in_specs=placed,
        out_specs=(
            P("tm", "space", None, None),
            P("tm", "space", None, None),
            P("tm", "space", None, None),
            P("tm", "space", None, None),
            P(),
        ),
        check_vma=False,
    )
```

profile of v0, /device:TPU:1, one launch (start us, length us, event | category | flops | bytes accessed | tf_op | source)
XLA Modules:
  0.0 849.6 jit_solution(3635706949680957188)
XLA Ops:
  7.2 2.0 reshape.94
  9.2 2.7 convert_reduce_fusion
  12.8 1.9 fusion.78
  14.8 119.5 %all-reduce.5.cloned.1.call-done = f32[2,20,112,112]{3,2,1,0:T(8,128)} async-done(((f32[2,20,112,112]{3,2,1,0:T(8,128)}), f32[2,20,112,112]{3,2,1,0:T(8,128)}) %all-reduce.5.cloned.1.call-update) | async-done | bytes 2007056 | tf_op jit(solution)/shard_map/psum | solution.py:78
  134.3 2.9 reduce_sum.137
  138.6 2.3 collective-permute-start.1
  140.8 3.3 collective-permute-start
  144.4 2.0 reshape.99
  148.6 44.8 %psum.36 = f32[2,20,112]{2,0,1:T(2,128)S(1)} all-reduce(f32[2,20,112]{2,0,1:T(2,128)S(1)} %copy.57), channel_id=1, replica_groups=mesh['tm'=16,'space'=16] {'space'}, use_global_device_ids=true, to_apply=%region_4.5 | all-reduce | flops 4480 | bytes 35840 | tf_op jit(solution)/shard_map/psum | solution.py:78
  193.5 22.7 %all-gather.4 = f32[16,20,112]{2,1,0:T(8,128)} all-gather(f32[1,20,112]{2,1,0:T(8,128)S(1)} %bitcast.88), channel_id=3, replica_groups=mesh['tm'=16,'space'=16] {'tm'}, dimensions={0}, use_global_device_ids=true | all-gather | bytes 152320 | tf_op jit(solution)/shard_map/all_gather | solution.py:33
  216.2 47.2 %all-gather.9.cloned.1.call-done = f32[320,112,112]{2,1,0:T(8,128)} async-done(((f32[20,112,112]{2,1,0:T(8,128)}), f32[320,112,112]{2,1,0:T(8,128)}) %all-gather.9.cloned.1.call-update) | async-done | bytes 16056336 | tf_op jit(solution)/shard_map/all_gather | solution.py:33
  264.9 3.7 fusion.82
  268.8 1.9 maximum_convert_fusion
  270.7 3.6 fusion.8
  274.5 1.6 stack.39
  276.4 140.1 %all-reduce.7.cloned.1.call-done = f32[2,20,112,112]{3,2,1,0:T(8,128)} async-done(((f32[2,20,112,112]{3,2,1,0:T(8,128)}), f32[2,20,112,112]{3,2,1,0:T(8,128)}) %all-reduce.7.cloned.1.call-update) | async-done | bytes 2007056 | tf_op jit(solution)/shard_map/psum | solution.py:105
  416.5 3.0 reduce_sum.142
  419.5 1.9 select_n.43
  421.4 1.9 select_n.45
  423.9 12.4 %add_convert_fusion = bf16[2,2,32,5632]{3,2,1,0:T(8,128)(2,1)} fusion(f32[2,4,32,5632]{3,2,1,0:T(8,128)} %copy-done, f32[5632]{0:T(1024)S(1)} %get-tuple-element.140, f32[5632]{0:T(1024)S(1)} %get-tuple-element.141, f32[5632]{0:T(1024)S(1)} %get-tuple-element.134, f32[5632]{0:T(1024)S(1)} %get-tuple-element.135, f32[5632]{0:T(1024)S(1)} %get-tuple-element.136, ...), kind=kLoop, calls=%fused_computation.29 | loop fusion | flops 12976128 | bytes 16062464 | tf_op jit(solution)/shard_map/convert_element_type | solution.py:144
  436.3 233.9 %all-reduce.9.cloned.1.call-done = f32[9,5632]{1,0:T(8,128)} async-done(((f32[9,5632]{1,0:T(8,128)}), f32[9,5632]{1,0:T(8,128)}) %all-reduce.9.cloned.1.call-update) | async-done | bytes 202768 | tf_op jit(solution)/shard_map/psum | solution.py:137
  670.2 1.8 broadcast_multiply_fusion
  672.0 6.7 fusion.48
  678.7 1.6 fusion.66
  680.4 2.8 fusion.54
  685.7 44.5 %psum.38 = f32[2,20,112]{2,0,1:T(2,128)S(1)} all-reduce(f32[2,20,112]{2,0,1:T(2,128)S(1)} %bitcast.87), channel_id=1, replica_groups=mesh['tm'=16,'space'=16] {'space'}, use_global_device_ids=true, to_apply=%region_11.12 | all-reduce | flops 4480 | bytes 35840 | tf_op jit(solution)/shard_map/psum | solution.py:105
  730.2 22.3 %all-gather.5 = f32[16,20,112]{2,1,0:T(8,128)} all-gather(f32[1,20,112]{2,1,0:T(8,128)S(1)} %bitcast.89), channel_id=5, replica_groups=mesh['tm'=16,'space'=16] {'tm'}, dimensions={0}, use_global_device_ids=true | all-gather | bytes 152320 | tf_op jit(solution)/shard_map/all_gather | solution.py:33
  752.5 43.3 %all-gather.11.cloned.1.call-done = f32[320,112,112]{2,1,0:T(8,128)} async-done(((f32[20,112,112]{2,1,0:T(8,128)}), f32[320,112,112]{2,1,0:T(8,128)}) %all-gather.11.cloned.1.call-update) | async-done | bytes 16056336 | tf_op jit(solution)/shard_map/all_gather | solution.py:33
  795.9 33.4 %while.27 = (s32[]{:T(128)}, f32[20,112,112]{2,1,0:T(8,128)S(1)}, f32[20,112]{1,0:T(8,128)S(1)}, s32[]{:T(128)}, f32[16,20,112,112]{3,2,1,0:T(8,128)}, /*index=5...) while((s32[]{:T(128)}, f32[20,112,112]{2,1,0:T(8,128)S(1)}, ...), condition=%wide.region_14.15_spmd, body=%wide.region_13.14_spmd.sunk | while | flops 253126 | bytes 3037603 | solution.py:42
  796.0 1.6 bitcast_add_fusion.10
  829.6 5.5 fusion.51
  836.8 2.5 fusion.57
  (128 shorter events, 47.1 us)
Async XLA Ops:
  7.2 127.1 %all-reduce.5.cloned.1.call-start = ((), (), s32[]{:S(2)}) async-start(), calls=%async_computation | async-start | bytes 4587520 | tf_op jit(solution)/shard_map/psum | solution.py:78
  9.2 5.5 copy-start.4
  12.8 1.9 copy-start.6
  14.8 122.6 %copy-start.3 = (bf16[2,2,32,5632]{3,2,1,0:T(8,128)(2,1)S(1)}, bf16[2,2,32,5632]{3,2,1,0:T(8,128)(2,1)}, u32[]{:S(2)}) copy-start(bf16[2,2,32,5632]{3,2,1,0:T(8,128)(2,1)} %param.18) | copy-start | bytes 4325380
  14.8 248.6 %all-gather.9.cloned.1.call-start = ((), (), s32[]{:S(2)}) async-start(), calls=%async_computation.3 | async-start | bytes 19496960 | tf_op jit(solution)/shard_map/all_gather | solution.py:33
  137.2 7.0 copy-start.22
  137.2 7.2 copy-start.17
  137.3 9.2 %copy-start.18 = (bf16[2,2,32,2240]{3,2,1,0:T(8,128)(2,1)S(1)}, bf16[2,2,32,2240]{3,2,1,0:T(8,128)(2,1)}, u32[]{:S(2)}) copy-start(bf16[2,2,32,2240]{3,2,1,0:T(8,128)(2,1)} %param.12) | copy-start | bytes 1720324
  137.3 279.2 %all-reduce.7.cloned.1.call-start = ((), (), s32[]{:S(2)}) async-start(), calls=%async_computation.1 | async-start | bytes 4587520 | tf_op jit(solution)/shard_map/psum | solution.py:105
  138.6 130.2 %collective-permute-start.1 = (bf16[2,1,32,5632]{3,2,1,0:T(8,128)(2,1)}, bf16[2,1,32,5632]{3,2,1,0:T(8,128)(2,1)}, u32[]{:S(2)}, u32[]{:S(2)}) collective-permute-start(bf16[2,1,32,5632]{3,2,1,0:T(8,128)(2,1)} %get-tuple-element.169), channel_id=1, source_target_pairs={{1,0},{2,1},{3,2},{4,3},{5,4},{6,5},{7,6},{8,7},{9,8},{10,9},{11,1... | collective-permute-start | bytes 2162696 | tf_op jit(solution)/shard_map/ppermute | solution.py:22
  140.8 127.9 %collective-permute-start = (bf16[2,1,32,5632]{3,2,1,0:T(8,128)(2,1)}, bf16[2,1,32,5632]{3,2,1,0:T(8,128)(2,1)}, u32[]{:S(2)}, u32[]{:S(2)}) collective-permute-start(bf16[2,1,32,5632]{3,2,1,0:T(8,128)(2,1)} %get-tuple-element.168), channel_id=1, source_target_pairs={{0,1},{1,2},{2,3},{3,4},{4,5},{5,6},{6,7},{7,8},{8,9},{9,10},{10,1... | collective-permute-start | bytes 2162696 | tf_op jit(solution)/shard_map/ppermute | solution.py:20
  148.6 116.3 %copy-start.14 = (bf16[2,64,20,112]{3,2,1,0:T(8,128)(2,1)}, bf16[2,64,20,112]{3,2,1,0:T(8,128)(2,1)S(1)}, u32[]{:S(2)}) copy-start(bf16[2,64,20,112]{3,2,1,0:T(8,128)(2,1)S(1)} %reshape.95) | copy-start | bytes 1720324
  263.8 4.8 copy-start.20
  268.7 401.5 %all-reduce.9.cloned.1.call-start = ((), (), s32[]{:S(2)}) async-start(), calls=%async_computation.2 | async-start | bytes 720896 | tf_op jit(solution)/shard_map/psum | solution.py:137
  268.7 1.9 copy-start.13
  270.6 3.6 copy-start
  276.2 143.3 %copy-start.9 = (f32[2,2,32,2240]{3,2,1,0:T(8,128)S(1)}, f32[2,2,32,2240]{3,2,1,0:T(8,128)}, u32[]{:S(2)}) copy-start(f32[2,2,32,2240]{3,2,1,0:T(8,128)} %get-tuple-element.172) | copy-start | bytes 3440644
  276.2 519.6 %all-gather.11.cloned.1.call-start = ((), (), s32[]{:S(2)}) async-start(), calls=%async_computation.4 | async-start | bytes 19496960 | tf_op jit(solution)/shard_map/all_gather | solution.py:33
  419.5 1.9 copy-start.10
  421.4 1.9 copy-start.19
  423.8 248.1 %copy-start.21 = (f32[2,20,112]{2,0,1:T(2,128)S(1)}, f32[2,20,112]{2,0,1:T(2,128)}, u32[]{:S(2)}) copy-start(f32[2,20,112]{2,0,1:T(2,128)} %copy-done.20) | copy-start | bytes 53764
  423.8 248.1 %copy-start.1 = (f32[2,20,112,112]{3,2,1,0:T(8,128)S(1)}, f32[2,20,112,112]{3,2,1,0:T(8,128)}, u32[]{:S(2)}) copy-start(f32[2,20,112,112]{3,2,1,0:T(8,128)} %all-reduce.5.cloned.1.call-done) | copy-start | bytes 6021124
  671.9 6.7 copy-start.11
  671.9 6.7 copy-start.15
  678.7 1.7 copy-start.12
  683.1 1.9 copy-start.16
  795.9 33.7 %copy-start.2 = (f32[2,20,112,112]{3,2,1,0:T(8,128)S(1)}, f32[2,20,112,112]{3,2,1,0:T(8,128)}, u32[]{:S(2)}) copy-start(f32[2,20,112,112]{3,2,1,0:T(8,128)} %all-reduce.7.cloned.1.call-done) | copy-start | bytes 6021124
  829.6 5.6 copy-start.7
  835.2 1.3 copy-start.5
  835.2 1.6 copy-start.8
Sparse Core Ops, SparseCore 0:
  14.9 119.3 all-reduce.4
  137.4 125.9 all-gather.8
  268.8 147.6 all-reduce.6
  422.5 247.6 all-reduce.8
  672.5 123.2 all-gather.10
where the time goes:
time: 851 us; the launch traced here: 850 us
  waiting for transfers between devices  584 us (69%)
  blocking collectives  134 us (16%)
  other arithmetic  63.2 us (7%)
  matrix products  28.2 us (3%)
  local copies, waits for them, and re-layouts  19.3 us (2%)
  between operations  14.3 us (2%)
    psum x1, waiting for transfers between devices, body(): kernel_total = lax.psum(jnp.stack(kernel_rows), ('tm', 'space'))  234 us
    psum x1, waiting for transfers between devices, body(): grad_states, grad_sums = lax.psum((grad_states, grad_sums), 'space')  140 us
    psum x1, waiting for transfers between devices, body(): states, sums = lax.psum((states, sums), 'space')  119 us
    all_gather x2, waiting for transfers between devices, prefix(): gathered = jax.tree.map(lambda a: lax.all_gather(a, axis), part)  90.5 us
    all_gather x2, blocking collectives, prefix(): gathered = jax.tree.map(lambda a: lax.all_gather(a, axis), part)  45 us
    psum x1, blocking collectives, body(): states, sums = lax.psum((states, sums), 'space')  44.8 us
    psum x1, blocking collectives, body(): grad_states, grad_sums = lax.psum((grad_states, grad_sums), 'space')  44.5 us
    add x30, other arithmetic, add_pair(): return (earlier[0] + later[0], earlier[1] + later[1])  33.3 us
  transfers between devices with their start and end apart: 7, of which 5 were waited for; matrix products, arithmetic and copies ran while one was open for 6% of the time, Pallas kernels for 0%

commit v1 on v0

--- a/solution.py
+++ b/solution.py
@@ -134,7 +134,7 @@
             window = padded[:, 2 - i : 2 - i + rows, 2 - j : 2 - j + cols]
             accum = accum + conv_weight[3 * i + j] * window
             kernel_rows.append(jnp.sum(window * input_wide, axis=(0, 1, 2)))
-    kernel_total = lax.psum(jnp.stack(kernel_rows), ("tm", "space"))
+    kernel_total = lax.psum(lax.psum(jnp.stack(kernel_rows), "tm"), "space")
     tokens_all = frames * rows * cols * lax.axis_size("tm") * lax.axis_size("space")
     kernel_grad = kernel_total * (1.0 / math.sqrt(tokens_all))
     return (

time: 851 us -> 665 us (0.78)
  waiting for transfers between devices: 584 us -> 393 us
    psum x1, waiting for transfers between devices: 234 us -> 90.7 us  [body(): kernel_total = lax.psum(lax.psum(jnp.stack(kernel_rows), 'tm'), 'space')]
    all_gather x2, waiting for transfers between devices: 90.5 us -> 63.6 us  [prefix(): gathered = jax.tree.map(lambda a: lax.all_gather(a, axis), part)]
    psum x1, waiting for transfers between devices: 140 us -> 119 us  [body(): grad_states, grad_sums = lax.psum((grad_states, grad_sums), 'space')]
  transfers between devices with their start and end apart: 7 -> 7, of which waited for: 5 -> 5; matrix products, arithmetic and copies ran while one was open for 6% -> 8% of each run, Pallas kernels for 0% -> 0%
where the time goes in v1:
time: 665 us; the launch traced here: 663 us
  waiting for transfers between devices  393 us (59%)
  blocking collectives  138 us (21%)
  other arithmetic  62.3 us (9%)
  matrix products  28.2 us (4%)
  local copies, waits for them, and re-layouts  20.9 us (3%)
  between operations  14.3 us (2%)
    psum x1, waiting for transfers between devices, body(): states, sums = lax.psum((states, sums), 'space')  119 us
    psum x1, waiting for transfers between devices, body(): grad_states, grad_sums = lax.psum((grad_states, grad_sums), 'space')  119 us
    psum x1, waiting for transfers between devices, body(): kernel_total = lax.psum(lax.psum(jnp.stack(kernel_rows), 'tm'), 'space')  90.7 us
    all_gather x2, waiting for transfers between devices, prefix(): gathered = jax.tree.map(lambda a: lax.all_gather(a, axis), part)  63.6 us
    psum x1, blocking collectives, body(): grad_states, grad_sums = lax.psum((grad_states, grad_sums), 'space')  47.8 us
    psum x1, blocking collectives, body(): states, sums = lax.psum((states, sums), 'space')  47.3 us
    all_gather x2, blocking collectives, prefix(): gathered = jax.tree.map(lambda a: lax.all_gather(a, axis), part)  43.1 us
    add x30, other arithmetic, add_pair(): return (earlier[0] + later[0], earlier[1] + later[1])  33.3 us
  transfers between devices with their start and end apart: 7, of which 5 were waited for; matrix products, arithmetic and copies ran while one was open for 8% of the time, Pallas kernels for 0%

profile of v1, /device:TPU:1, one launch (start us, length us, event | category | flops | bytes accessed | tf_op | source)
XLA Modules:
  0.0 662.8 jit_solution(1198470423613572809)
XLA Ops:
  7.2 2.0 reshape.94
  9.2 2.7 convert_reduce_fusion
  12.8 1.9 fusion.78
  14.8 119.5 %all-reduce.6.cloned.1.call-done = f32[2,20,112,112]{3,2,1,0:T(8,128)} async-done(((f32[2,20,112,112]{3,2,1,0:T(8,128)}), f32[2,20,112,112]{3,2,1,0:T(8,128)}) %all-reduce.6.cloned.1.call-update) | async-done | bytes 2007056 | tf_op jit(solution)/shard_map/psum | solution.py:78
  134.3 3.0 reduce_sum.137
  138.5 1.9 collective-permute-start
  140.5 3.3 collective-permute-start.1
  143.9 1.9 reshape.99
  147.2 1.7 reshape.95
  149.0 47.3 %psum.43 = f32[2,20,112]{2,0,1:T(2,128)S(1)} all-reduce(f32[2,20,112]{2,0,1:T(2,128)S(1)} %copy.57), channel_id=1, replica_groups=mesh['tm'=16,'space'=16] {'space'}, use_global_device_ids=true, to_apply=%region_4.5 | all-reduce | flops 4480 | bytes 35840 | tf_op jit(solution)/shard_map/psum | solution.py:78
  196.4 21.1 %all-gather.4 = f32[16,20,112]{2,1,0:T(8,128)S(1)} all-gather(f32[1,20,112]{2,1,0:T(8,128)S(1)} %bitcast.88), channel_id=3, replica_groups=mesh['tm'=16,'space'=16] {'tm'}, dimensions={0}, use_global_device_ids=true | all-gather | bytes 152320 | tf_op jit(solution)/shard_map/all_gather | solution.py:33
  217.6 1.9 maximum_convert_fusion
  219.5 3.6 fusion.8
  223.3 1.6 stack.39
  225.0 38.4 %all-gather.9.cloned.1.call-done = f32[320,112,112]{2,1,0:T(8,128)} async-done(((f32[20,112,112]{2,1,0:T(8,128)}), f32[320,112,112]{2,1,0:T(8,128)}) %all-gather.9.cloned.1.call-update) | async-done | bytes 16056336 | tf_op jit(solution)/shard_map/all_gather | solution.py:33
  265.7 3.7 fusion.82
  269.5 90.7 %all-reduce.8.cloned.1.call-done = f32[9,5632]{1,0:T(8,128)} async-done(((f32[9,5632]{1,0:T(8,128)}), f32[9,5632]{1,0:T(8,128)}) %all-reduce.8.cloned.1.call-update) | async-done | bytes 202768 | tf_op jit(solution)/shard_map/psum | solution.py:137
  360.5 119.1 %all-reduce.10.cloned.1.call-done = (f32[2,20,112,112]{3,2,1,0:T(8,128)}, f32[9,5632]{1,0:T(8,128)}) async-done(((f32[2,20,112,112]{3,2,1,0:T(8,128)}, f32[9,5632]{1,0:T(8,128)}), (f32[2,20,112,112]{3,2,1,0:T(8,128)}, f32[9,5632]{1,0:T(8,128)})) %all-reduce.10.cloned.1.call-update) | async-done | bytes 2209808 | tf_op jit(solution)/shard_map/psum | solution.py:105
  479.6 3.0 reduce_sum.142
  482.5 1.9 select_n.43
  484.4 2.0 select_n.45
  487.0 12.4 %add_convert_fusion = bf16[2,2,32,5632]{3,2,1,0:T(8,128)(2,1)} fusion(f32[2,4,32,5632]{3,2,1,0:T(8,128)} %copy-done, f32[5632]{0:T(1024)S(1)} %get-tuple-element.140, f32[5632]{0:T(1024)S(1)} %get-tuple-element.141, f32[5632]{0:T(1024)S(1)} %get-tuple-element.134, f32[5632]{0:T(1024)S(1)} %get-tuple-element.135, f32[5632]{0:T(1024)S(1)} %get-tuple-element.136, ...), kind=kLoop, calls=%fused_computation.29 | loop fusion | flops 12976128 | bytes 16062464 | tf_op jit(solution)/shard_map/convert_element_type | solution.py:144
  499.4 6.7 %fusion.48 = f32[2,20,112,112]{3,0,2,1:T(2,128)S(1)} fusion(f32[2,20,112,112]{3,2,1,0:T(8,128)S(1)} %copy-done.1, f32[20,112,112]{2,1,0:T(8,128)S(1)} %get-tuple-element.120, s32[2]{0:T(128)S(1)} %bitcast.96), kind=kOutput, calls=%fused_computation.57 | convolution fusion | flops 12544004 | bytes 5017608 | tf_op jit(solution)/shard_map/fg,ghde->fhde/dot_general | solution.py:86
  506.2 1.6 fusion.66
  508.5 2.8 fusion.54
  513.1 47.8 %psum.45 = f32[2,20,112]{2,0,1:T(2,128)S(1)} all-reduce(f32[2,20,112]{2,0,1:T(2,128)S(1)} %bitcast.87), channel_id=1, replica_groups=mesh['tm'=16,'space'=16] {'space'}, use_global_device_ids=true, to_apply=%region_11.12 | all-reduce | flops 4480 | bytes 35840 | tf_op jit(solution)/shard_map/psum | solution.py:105
  560.9 21.9 %all-gather.5 = f32[16,20,112]{2,1,0:T(8,128)} all-gather(f32[1,20,112]{2,1,0:T(8,128)S(1)} %bitcast.89), channel_id=5, replica_groups=mesh['tm'=16,'space'=16] {'tm'}, dimensions={0}, use_global_device_ids=true | all-gather | bytes 152320 | tf_op jit(solution)/shard_map/all_gather | solution.py:33
  583.6 25.2 %all-gather.11.cloned.1.call-done = f32[320,112,112]{2,1,0:T(8,128)} async-done(((f32[20,112,112]{2,1,0:T(8,128)}), f32[320,112,112]{2,1,0:T(8,128)}) %all-gather.11.cloned.1.call-update) | async-done | bytes 16056336 | tf_op jit(solution)/shard_map/all_gather | solution.py:33
  608.9 33.7 %while.27 = (s32[]{:T(128)}, f32[20,112,112]{2,1,0:T(8,128)S(1)}, f32[20,112]{1,0:T(8,128)S(1)}, s32[]{:T(128)}, f32[16,20,112,112]{3,2,1,0:T(8,128)}, /*index=5...) while((s32[]{:T(128)}, f32[20,112,112]{2,1,0:T(8,128)S(1)}, ...), condition=%wide.region_14.15_spmd, body=%wide.region_13.14_spmd.sunk | while | flops 253126 | bytes 3037603 | solution.py:42
  609.8 1.5 bitcast_add_fusion.10
  642.8 5.5 fusion.51
  650.0 2.5 fusion.57
  (124 shorter events, 48.0 us)
Async XLA Ops:
  7.2 127.1 %all-reduce.6.cloned.1.call-start = ((), (), s32[]{:S(2)}) async-start(), calls=%async_computation | async-start | bytes 4587520 | tf_op jit(solution)/shard_map/psum | solution.py:78
  9.2 5.5 copy-start.4
  12.8 1.9 copy-start.6
  14.8 122.6 %copy-start.3 = (bf16[2,2,32,5632]{3,2,1,0:T(8,128)(2,1)S(1)}, bf16[2,2,32,5632]{3,2,1,0:T(8,128)(2,1)}, u32[]{:S(2)}) copy-start(bf16[2,2,32,5632]{3,2,1,0:T(8,128)(2,1)} %param.18) | copy-start | bytes 4325380
  14.8 248.6 %all-gather.9.cloned.1.call-start = ((), (), s32[]{:S(2)}) async-start(), calls=%async_computation.2 | async-start | bytes 19496960 | tf_op jit(solution)/shard_map/all_gather | solution.py:33
  137.2 6.5 copy-start.20
  137.2 6.7 %copy-start.15 = (bf16[2,2,32,2240]{3,2,1,0:T(8,128)(2,1)S(1)}, bf16[2,2,32,2240]{3,2,1,0:T(8,128)(2,1)}, u32[]{:S(2)}) copy-start(bf16[2,2,32,2240]{3,2,1,0:T(8,128)(2,1)} %param.15) | copy-start | bytes 1720324
  137.3 222.9 %all-reduce.8.cloned.1.call-start = ((), (), s32[]{:S(2)}) async-start(), calls=%async_computation.1 | async-start | bytes 720896 | tf_op jit(solution)/shard_map/psum | solution.py:137
  138.5 79.0 %collective-permute-start = (bf16[2,1,32,5632]{3,2,1,0:T(8,128)(2,1)}, bf16[2,1,32,5632]{3,2,1,0:T(8,128)(2,1)}, u32[]{:S(2)}, u32[]{:S(2)}) collective-permute-start(bf16[2,1,32,5632]{3,2,1,0:T(8,128)(2,1)} %get-tuple-element.170), channel_id=1, source_target_pairs={{0,1},{1,2},{2,3},{3,4},{4,5},{5,6},{6,7},{7,8},{8,9},{9,10},{10,1... | collective-permute-start | bytes 2162696 | tf_op jit(solution)/shard_map/ppermute | solution.py:20
  140.5 77.1 %collective-permute-start.1 = (bf16[2,1,32,5632]{3,2,1,0:T(8,128)(2,1)}, bf16[2,1,32,5632]{3,2,1,0:T(8,128)(2,1)}, u32[]{:S(2)}, u32[]{:S(2)}) collective-permute-start(bf16[2,1,32,5632]{3,2,1,0:T(8,128)(2,1)} %get-tuple-element.171), channel_id=1, source_target_pairs={{1,0},{2,1},{3,2},{4,3},{5,4},{6,5},{7,6},{8,7},{9,8},{10,9},{11,1... | collective-permute-start | bytes 2162696 | tf_op jit(solution)/shard_map/ppermute | solution.py:22
  217.5 1.9 copy-start.12
  219.4 3.6 copy-start
  225.0 254.6 %all-reduce.10.cloned.1.call-start = ((), (), s32[]{:S(2)}) async-start(), calls=%async_computation.4 | async-start | bytes 5308416 | tf_op jit(solution)/shard_map/psum | solution.py:105
  263.5 1.1 copy-start.13
  263.8 5.6 copy-start.18
  360.2 248.6 %all-gather.11.cloned.1.call-start = ((), (), s32[]{:S(2)}) async-start(), calls=%async_computation.3 | async-start | bytes 19496960 | tf_op jit(solution)/shard_map/all_gather | solution.py:33
  482.5 1.9 copy-start.9
  484.4 2.0 copy-start.17
  486.9 12.4 %copy-start.19 = (f32[2,20,112]{2,0,1:T(2,128)S(1)}, f32[2,20,112]{2,0,1:T(2,128)}, u32[]{:S(2)}) copy-start(f32[2,20,112]{2,0,1:T(2,128)} %copy-done.18) | copy-start | bytes 53764
  487.0 12.4 %copy-start.1 = (f32[2,20,112,112]{3,2,1,0:T(8,128)S(1)}, f32[2,20,112,112]{3,2,1,0:T(8,128)}, u32[]{:S(2)}) copy-start(f32[2,20,112,112]{3,2,1,0:T(8,128)} %all-reduce.6.cloned.1.call-done) | copy-start | bytes 6021124
  499.4 6.7 %copy-start.10 = (f32[2,64,20,112]{3,2,1,0:T(8,128)S(1)}, f32[2,64,20,112]{3,2,1,0:T(8,128)}, u32[]{:S(2)}) copy-start(f32[2,64,20,112]{3,2,1,0:T(8,128)} %reshape.99) | copy-start | bytes 3440644
  499.4 6.7 %copy-start.14 = (bf16[2,64,20,112]{3,2,1,0:T(8,128)(2,1)S(1)}, bf16[2,64,20,112]{3,2,1,0:T(8,128)(2,1)}, u32[]{:S(2)}) copy-start(bf16[2,64,20,112]{3,2,1,0:T(8,128)(2,1)} %reshape.95) | copy-start | bytes 1720324
  506.2 2.3 copy-start.11
  511.2 71.6 %copy-start.16 = (f32[9,5632]{1,0:T(8,128)S(1)}, f32[9,5632]{1,0:T(8,128)}, u32[]{:S(2)}) copy-start(f32[9,5632]{1,0:T(8,128)} %get-tuple-element.167) | copy-start | bytes 608260
  608.9 33.9 %copy-start.2 = (f32[2,20,112,112]{3,2,1,0:T(8,128)S(1)}, f32[2,20,112,112]{3,2,1,0:T(8,128)}, u32[]{:S(2)}) copy-start(f32[2,20,112,112]{3,2,1,0:T(8,128)} %get-tuple-element.166) | copy-start | bytes 6021124
  642.8 5.6 copy-start.7
  648.4 1.3 copy-start.5
  648.4 1.6 copy-start.8
Sparse Core Ops, SparseCore 0:
  14.9 119.3 all-reduce.5
  137.4 125.9 all-gather.8
  267.2 92.9 all-reduce.7
  362.5 116.9 all-reduce.9
  482.7 126.0 all-gather.10
